TPU v7x, 32 devices: a whole 2x2x4 slice. The times are simulated.
32 devices in a mesh: mech: 8 (over z, x), bin: 4 (over y, core).
Axes of the slice: x: 2, y: 2, z: 4, core: 2. Of those that a mesh axis runs over, the one named last changes fastest.
Arguments:
- face_coords: float32 [27, 65536], P(None, ('mech', 'bin')), may hold values from -1.03 to 1.03, as said below
- face_stiff: float32 [65536], P(('mech', 'bin')), may hold values from 1 to 10
- bin_order: int32 [32, 2048], P(('mech', 'bin')), may hold values from 0 to 2047, each once within a row
- slave_pos: float32 [3, 131072], P(None, ('mech', 'bin')), may hold values from -1.3 to 1.3, as said below
- slave_dest: int32 [131072, 1], P(('mech', 'bin')), may hold values from 0 to 31, as said below
- face_slot: int32 [131072], P(('mech', 'bin')), may hold values from 0 to 2047
- block_count: int32 [32, 32], P(('mech', 'bin')), may hold values from 64 to 128
- mirror_face: int32 [65536], P(('mech', 'bin')), may hold values from 0 to 2047
- mirror_node: int32 [65536], P(('mech', 'bin')), may hold values from 0 to 8
- mirror_dest: int32 [65536, 1], P(('mech', 'bin')), may hold values from 0 to 31, as said below
- mirror_slot: int32 [65536], P(('mech', 'bin')), may hold values from 0 to 2047
Outputs:
- slave_force: float32 [3, 131072], P(None, ('mech', 'bin'))
- face_force: float32 [27, 65536], P(None, ('mech', 'bin'))
Inputs may be any that keep to these rules, and one draw needn't show every extreme that they name: `face_coords`: node a = i + 3 j of every face lies within 0.03 of (i - 1, j - 1) in its first two components; its third component lies in -0.35 to 0.35. `slave_pos`: first two components lie in -1.3 to 1.3, the third in -0.6 to 0.6. `slave_dest`: among the rows of one device, no bin device is named by more than 256 rows, no element owner holds the named faces of more than 256 rows, and no bin device together with one owner by more than 256 // 4 rows; some bin device and some owner reach 256 from every device. `mirror_dest`: among the rows of one device, no partner device is named by more than 128 rows, no element owner holds the named faces of more than 128 rows, and no partner device together with one owner by more than 128 // 4 rows; some partner device and some owner reach 128 from every device. `bin_order`: each row is a permutation of 0 to 2047.
All inputs are finite; a program needn't handle non-finite values.
Results may differ from a plain program's by a relative error of at most 0.0003.
Values sent between devices are 32-bit elements; how exact they have to be, the bound alone decides.
A program may use at most 64 MiB of HBM per device.

v0:
```python
import functools

import jax
import jax.numpy as jnp
from jax import lax
from jax.experimental import pallas as pl
from jax.experimental.pallas import tpu as pltpu
from jax.sharding import PartitionSpec as P

NEWTON = 5
CLIP_EDGE = 1.1
LANES = 128
LOW = 256
F32 = jnp.float32
BF16 = jnp.bfloat16


def iota(shape, axis):
    return lax.broadcasted_iota(jnp.int32, shape, axis)


def whole_part(value, size):
    return jnp.floor((value + 0.5) * (1.0 / size))


def pieces(value):
    high = value.astype(BF16).astype(F32)
    return high, value - high


def hot(mask):
    return jnp.where(mask, 1.0, 0.0).astype(BF16)


def dot_lanes(left, right):
    return lax.dot_general(left, right, (((1,), (1,)), ((), ())), preferred_element_type=F32)


def dot_plain(left, right):
    return lax.dot_general(left, right, (((1,), (0,)), ((), ())), preferred_element_type=F32)


def owner_of(dest, slot, n_bin, block_faces):
    dest = dest.astype(F32)
    slot = slot.astype(F32)
    group = whole_part(dest, n_bin)
    part = whole_part(slot, block_faces)
    owner = group * n_bin + part
    place = (dest - group * n_bin) * block_faces + slot - part * block_faces
    return owner, place


def rank_chunk(owner, seen, tri):
    devices = seen.shape[0]
    width = owner.shape[1]
    mask = iota((devices, width), 0) == owner.astype(jnp.int32)
    ones = jnp.where(mask, 1.0, 0.0)
    earlier = dot_plain(ones.astype(BF16), tri)
    rank = jnp.sum(jnp.where(mask, earlier + seen, 0.0), 0, keepdims=True)
    return rank, seen + jnp.sum(ones, 1, keepdims=True)


def by_group(key, rows8, groups):
    width = rows8.shape[1]
    group = (iota((4 * groups, width), 0) >> 2).astype(F32)
    return jnp.where(group == key, jnp.concatenate([rows8] * (groups // 2), 0), 0.0)


def spread(key, lane, point, index, groups, lanes):
    width = key.shape[1]
    row = iota((8, width), 0) & 3
    rows8 = jnp.where(
        row == 0, point[0], jnp.where(row == 1, point[1], jnp.where(row == 2, point[2], index))
    )
    onehot = hot(iota((lanes, width), 0) == lane.astype(jnp.int32))
    high, low = pieces(rows8)
    return dot_lanes(by_group(key, high, groups).astype(BF16), onehot) + dot_lanes(
        by_group(key, low, groups).astype(BF16), onehot
    )


def dispatch(n_bin, ratio, count, pos, sdest, sslot, send, info_s, faces):
    faces_bin = faces // n_bin
    devices = send.shape[0]
    slaves = pos.shape[1]
    width = 256
    tri = hot(iota((width, width), 0) < iota((width, width), 1))
    seen = jnp.zeros((devices, 1), F32)
    total = jnp.zeros((4 * ratio * devices, LANES), F32)
    for step in range(slaves // width):
        cols = pl.ds(step * width, width)
        owner, place = owner_of(sdest[:, cols], sslot[:, cols], n_bin, faces_bin)
        spot = iota((1, width), 1)
        limit = jnp.where(
            spot < 128,
            count[0:1, 2 * step : 2 * step + 1],
            count[0:1, 2 * step + 1 : 2 * step + 2],
        )
        live = (spot & 127) < limit
        owner = jnp.where(live, owner, -1.0)
        rank, seen = rank_chunk(owner, seen, tri)
        over = whole_part(rank, LANES)
        key = jnp.where(live, owner * ratio + over, -1.0)
        lane = rank - over * LANES
        info_s[0:1, cols] = key
        info_s[1:2, cols] = lane
        point = [pos[c : c + 1, cols] for c in range(3)]
        total = total + spread(key, lane, point, place + 1.0, ratio * devices, LANES)
    send[:, 0 : 4 * ratio, :] = total.reshape(devices, 4 * ratio, LANES)


def dispatch_mirrors(n_bin, ratio, coords, mface, mnode, mdest, mslot, send, info_m):
    faces = coords.shape[1]
    devices = send.shape[0]
    mirrors = mface.shape[1]
    width = 256
    tri = hot(iota((width, width), 0) < iota((width, width), 1))
    high_count = faces // LOW
    coord_pieces = pieces(coords[...])
    table = jnp.concatenate(
        [
            jnp.concatenate(
                [
                    jnp.pad(piece[:, h * LOW : (h + 1) * LOW], ((0, 5), (0, 0))).astype(BF16)
                    for h in range(high_count)
                ],
                0,
            )
            for piece in coord_pieces
        ],
        1,
    )
    seen = jnp.zeros((devices, 1), F32)
    total = jnp.zeros((4 * devices, LANES), F32)
    row = iota((32, width), 0)
    for step in range(mirrors // width):
        cols = pl.ds(step * width, width)
        owner, place = owner_of(mdest[:, cols], mslot[:, cols], n_bin, faces // n_bin)
        rank, seen = rank_chunk(owner, seen, tri)
        info_m[0:1, cols] = owner
        info_m[1:2, cols] = rank
        face = mface[:, cols]
        onehot = hot(iota((LOW, width), 0) == (face & (LOW - 1)))
        found = dot_plain(table, jnp.concatenate([onehot, onehot], 0))
        part = face >> 8
        nodes = jnp.zeros((32, width), F32)
        for h in range(high_count):
            nodes = jnp.where(part == h, found[32 * h : 32 * h + 32], nodes)
        first = 3 * mnode[:, cols]
        point = [
            jnp.sum(jnp.where(row == first + c, nodes, 0.0), 0, keepdims=True) for c in range(3)
        ]
        total = total + spread(owner, rank, point, place + 1.0, devices, LANES)
    send[:, 4 * ratio : 4 * ratio + 4, :] = total.reshape(devices, 4, LANES)


def lagrange(t):
    return (
        (t * (t - 1.0) * 0.5, 1.0 - t * t, t * (t + 1.0) * 0.5),
        (t - 0.5, -2.0 * t, t + 0.5),
    )


def surface(nodes, u, v):
    val_u, slope_u = lagrange(u)
    val_v, slope_v = lagrange(v)
    at, along_u, along_v = [], [], []
    for c in range(3):
        line = [sum(val_u[i] * nodes[3 * (i + 3 * j) + c] for i in range(3)) for j in range(3)]
        slope = [sum(slope_u[i] * nodes[3 * (i + 3 * j) + c] for i in range(3)) for j in range(3)]
        at.append(sum(val_v[j] * line[j] for j in range(3)))
        along_u.append(sum(val_v[j] * slope[j] for j in range(3)))
        along_v.append(sum(slope_v[j] * line[j] for j in range(3)))
    return val_u, val_v, at, along_u, along_v


def inner(a, b):
    return a[0] * b[0] + a[1] * b[1] + a[2] * b[2]


def contact(point, nodes, stiff):
    u = jnp.zeros_like(point[0])
    v = jnp.zeros_like(point[0])
    for _ in range(NEWTON):
        _, _, at, tu, tv = surface(nodes, u, v)
        off = [point[c] - at[c] for c in range(3)]
        a_uu, a_uv, a_vv = inner(tu, tu), inner(tu, tv), inner(tv, tv)
        b_u, b_v = inner(tu, off), inner(tv, off)
        inv = 1.0 / (a_uu * a_vv - a_uv * a_uv)
        u = jnp.clip(u + (a_vv * b_u - a_uv * b_v) * inv, -CLIP_EDGE, CLIP_EDGE)
        v = jnp.clip(v + (a_uu * b_v - a_uv * b_u) * inv, -CLIP_EDGE, CLIP_EDGE)
    val_u, val_v, at, tu, tv = surface(nodes, u, v)
    normal = [
        tu[1] * tv[2] - tu[2] * tv[1],
        tu[2] * tv[0] - tu[0] * tv[2],
        tu[0] * tv[1] - tu[1] * tv[0],
    ]
    scale = 1.0 / jnp.sqrt(inner(normal, normal))
    normal = [n * scale for n in normal]
    off = [point[c] - at[c] for c in range(3)]
    press = 0.5 * stiff * jnp.maximum(-inner(off, normal), 0.0)
    force = [press * n for n in normal]
    return force, val_u, val_v


def lookup(ref, row, low, high):
    result = None
    for h in range(ref.shape[1] // LANES):
        line = jnp.broadcast_to(ref[row : row + 1, h * LANES : (h + 1) * LANES], (8, LANES))
        value = jnp.take_along_axis(line, low, axis=1, mode="promise_in_bounds")
        result = value if h == 0 else jnp.where(high == h, value, result)
    return result


def contact_block(first, dense, rows, order, coords, stiff, recv, ret, react, found, slot):
    def far(c):
        return pl.ds(first + c, 8, stride=slot)

    point = [recv[far(c), :] for c in range(3)]
    code = recv[far(3), :]
    place = jnp.maximum(code - 1.0, 0.0).astype(jnp.int32)
    face = lookup(order, 0, place & (LANES - 1), place >> 7)
    low, high = face & (LANES - 1), face >> 7
    nodes = [lookup(coords, r, low, high) for r in range(27)]
    strength = jnp.where(code > 0.5, lookup(stiff, 0, low, high), 0.0)
    found[pl.ds(dense, 8), :] = face
    force, val_u, val_v = contact(point, nodes, strength)
    for c in range(3):
        ret[far(c), :] = force[c]
    ret[far(3), :] = jnp.zeros_like(code)
    for j in range(3):
        for i in range(3):
            weight = -(val_u[i] * val_v[j])
            for c in range(3):
                row = 3 * (i + 3 * j) + c
                react[pl.ds(row * rows + dense, 8), :] = weight * force[c]


def scatter(rows, high_count, react, found, total):
    total[...] = jnp.zeros_like(total)

    def add(i, carry):
        lefts, rights = [], []
        for q in range(8):
            p = i * 8 + q
            value = react[pl.ds(p, 32, stride=rows), :]
            upper, lower = pieces(value)
            both = jnp.concatenate([upper.astype(BF16), lower.astype(BF16)], 0)
            face = found[pl.ds(p, 1), :]
            high = jnp.broadcast_to(face >> 8, (16, LANES))
            parts = []
            for h in range(high_count):
                mask = hot(high == h)
                parts.append(both * jnp.concatenate([mask] * 4, 0))
            lefts.append(jnp.concatenate(parts, 0))
            rights.append(hot(iota((LOW, LANES), 0) == (face & (LOW - 1))))
        total[...] += dot_lanes(jnp.concatenate(lefts, 1), jnp.concatenate(rights, 1))
        return carry

    lax.fori_loop(0, rows // 8, add, 0)


def fetch(key, lane, table, groups):
    width = key.shape[1]
    onehot = hot(iota((LANES, width), 0) == lane.astype(jnp.int32))
    spreaded = dot_plain(table, jnp.concatenate([onehot, onehot], 0))
    group = (iota((4 * groups, width), 0) >> 2).astype(F32)
    spreaded = jnp.where(group == key, spreaded, 0.0)
    result = jnp.sum(spreaded.reshape(groups // 2, 8, width), 0)
    return result + pltpu.roll(result, 4, 0)


def piece_table(value):
    return jnp.concatenate([p.astype(BF16) for p in pieces(value)], 1)


def collect(ratio, info_s, info_m, mface, mnode, back, slave_force, face_force, total, own):
    devices = back.shape[0]
    slaves = info_s.shape[1]
    mirrors = info_m.shape[1]
    high_count = face_force.shape[1] // LOW
    width = 256
    table = piece_table(back[:, 4 * ratio : 4 * ratio + 4, :].reshape(4 * devices, LANES))
    acc = None
    for step in range(mirrors // width):
        cols = pl.ds(step * width, width)
        result = fetch(info_m[0:1, cols], info_m[1:2, cols], table, devices)
        face = mface[:, cols]
        key = (face >> 8) * 16 + mnode[:, cols]
        rel = jnp.broadcast_to(key, (8, width)) - (iota((8, width), 0) >> 2)
        left = []
        for piece in pieces(result):
            for h in range(high_count):
                for j in range(5):
                    left.append(jnp.where(rel == 16 * h + 2 * j, piece, 0.0))
        left = jnp.concatenate(left, 0).astype(BF16)
        onehot = hot(iota((LOW, width), 0) == (face & (LOW - 1)))
        term = dot_lanes(left, onehot)
        acc = term if acc is None else acc + term
    own[...] = acc
    half = 40 * high_count
    for h in range(high_count):
        cols = slice(h * LOW, (h + 1) * LOW)
        mine = own[40 * h : 40 * h + 40, :] + own[half + 40 * h : half + 40 * h + 40, :]
        sent = total[64 * h : 64 * h + 27, :] + total[64 * h + 32 : 64 * h + 59, :]
        for n in range(9):
            face_force[3 * n : 3 * n + 3, cols] = (
                sent[3 * n : 3 * n + 3] + mine[4 * n : 4 * n + 3]
            )
    table = piece_table(back[:, 0 : 4 * ratio, :].reshape(4 * ratio * devices, LANES))
    for step in range(slaves // width):
        cols = pl.ds(step * width, width)
        result = fetch(info_s[0:1, cols], info_s[1:2, cols], table, devices * ratio)
        slave_force[:, cols] = result[0:3]


def step_kernel(n_mech, n_bin, ratio, *refs):
    inputs, (slave_force, face_force) = refs[:11], refs[11:13]
    local, rest = refs[13:24], refs[24:]
    (
        send, recv, ret, back, info_s, info_m, react, found, total, own,
        load_sem, go_send, go_recv, home_send, home_recv,
    ) = rest
    devices = n_mech * n_bin
    slot = send.shape[1]
    used = 4 * (ratio + 1)
    rows = (ratio + 1) * devices
    me = lax.axis_index("mech") * n_bin + lax.axis_index("bin")

    def device(i):
        return (i // n_bin, lax.rem(i, n_bin))

    barrier = pltpu.get_barrier_semaphore()

    def greet(i, carry):
        pl.semaphore_signal(
            barrier,
            inc=1,
            device_id=device(lax.rem(me + i, devices)),
            device_id_type=pl.DeviceIdType.MESH,
        )
        return carry

    loads = [
        pltpu.make_async_copy(inputs[n], local[n], load_sem.at[n]) for n in range(len(inputs))
    ]
    for load in loads:
        load.start()
    lax.fori_loop(1, devices, greet, 0)
    (count, pos, sdest, sslot, coords, mface, mnode, mdest, mslot, order, stiff) = local
    faces = coords.shape[1]
    for load in loads:
        load.wait()
    dispatch(n_bin, ratio, count, pos, sdest, sslot, send, info_s, faces)
    dispatch_mirrors(n_bin, ratio, coords, mface, mnode, mdest, mslot, send, info_m)
    pl.semaphore_wait(barrier, devices - 1)

    def go(i):
        target = lax.rem(me + i, devices)
        return pltpu.make_async_remote_copy(
            src_ref=send.at[target, pl.ds(0, used), :],
            dst_ref=recv.at[pl.ds(pl.multiple_of(i * slot, slot), used), :],
            send_sem=go_send.at[i],
            recv_sem=go_recv.at[i],
            device_id=device(target),
            device_id_type=pl.DeviceIdType.MESH,
        )

    def home(i):
        target = lax.rem(me - i + devices, devices)
        return pltpu.make_async_remote_copy(
            src_ref=ret.at[pl.ds(pl.multiple_of(i * slot, slot), used), :],
            dst_ref=back.at[me, pl.ds(0, used), :],
            send_sem=home_send.at[i],
            recv_sem=home_recv.at[i],
            device_id=device(target),
            device_id_type=pl.DeviceIdType.MESH,
        )

    def start_go(i, carry):
        go(i).start()
        return carry

    lax.fori_loop(1, devices, start_go, 0)
    recv[0:used, :] = send[me, 0:used, :]
    react[pl.ds(27 * rows, 5 * rows), :] = jnp.zeros((5 * rows, LANES), F32)

    def group(j, carry):
        for q in range(8):
            i = j * 8 + q

            @pl.when(i > 0)
            def _():
                go(i).wait_recv()

        def block(k, inside):
            first = j * (8 * slot) + 4 * k
            dense = pl.multiple_of((j * (ratio + 1) + k) * 8, 8)
            contact_block(
                first, dense, rows, order, coords, stiff, recv, ret, react, found, slot
            )
            return inside

        lax.fori_loop(0, ratio + 1, block, 0)
        for q in range(8):
            i = j * 8 + q

            @pl.when(i > 0)
            def _():
                home(i).start()

        return carry

    lax.fori_loop(0, devices // 8, group, 0)
    back[me, 0:used, :] = ret[0:used, :]
    scatter(rows, faces // LOW, react, found, total)

    def finish(i, carry):
        go(i).wait_send()
        home(i).wait_send()
        home(i).wait_recv()
        return carry

    lax.fori_loop(1, devices, finish, 0)
    collect(ratio, info_s, info_m, mface, mnode, back, slave_force, face_force, total, own)


def shards(
    face_coords,
    face_stiff,
    bin_order,
    slave_pos,
    slave_dest,
    face_slot,
    block_count,
    mirror_face,
    mirror_node,
    mirror_dest,
    mirror_slot,
):
    n_mech = lax.axis_size("mech")
    n_bin = lax.axis_size("bin")
    devices = n_mech * n_bin
    slaves = slave_pos.shape[1]
    mirrors = mirror_face.shape[0]
    faces = face_coords.shape[1]
    cap = 2 * slaves // devices
    ratio = -(-cap // LANES)
    rows = (ratio + 1) * devices
    slot = 8 * (-(-(ratio + 1) // 2))
    high_count = faces // LOW
    operands = (
        block_count,
        slave_pos,
        slave_dest.reshape(1, slaves),
        face_slot.reshape(1, slaves),
        face_coords,
        mirror_face.reshape(1, mirrors),
        mirror_node.reshape(1, mirrors),
        mirror_dest.reshape(1, mirrors),
        mirror_slot.reshape(1, mirrors),
        bin_order,
        face_stiff.reshape(1, faces),
    )
    vmem = pl.BlockSpec(memory_space=pltpu.VMEM)
    return pl.pallas_call(
        functools.partial(step_kernel, n_mech, n_bin, ratio),
        out_shape=(
            jax.ShapeDtypeStruct((3, slaves), F32),
            jax.ShapeDtypeStruct((27, faces), F32),
        ),
        in_specs=[pl.BlockSpec(memory_space=pltpu.HBM)] * len(operands),
        out_specs=(vmem, vmem),
        scratch_shapes=[pltpu.VMEM(o.shape, o.dtype) for o in operands]
        + [
            pltpu.VMEM((devices, slot, LANES), F32),
            pltpu.VMEM((devices * slot, LANES), F32),
            pltpu.VMEM((devices * slot, LANES), F32),
            pltpu.VMEM((devices, slot, LANES), F32),
            pltpu.VMEM((2, slaves), F32),
            pltpu.VMEM((2, mirrors), F32),
            pltpu.VMEM((32 * rows, LANES), F32),
            pltpu.VMEM((rows, LANES), jnp.int32),
            pltpu.VMEM((64 * high_count, LOW), F32),
            pltpu.VMEM((80 * high_count, LOW), F32),
            pltpu.SemaphoreType.DMA((len(operands),)),
        ]
        + [pltpu.SemaphoreType.DMA((devices,))] * 4,
        compiler_params=pltpu.CompilerParams(
            vmem_limit_bytes=48 * 2**20, collective_id=0, has_side_effects=True
        ),
        name="contact_step",
    )(*operands)


def solution(mesh):
    both = ("mech", "bin")
    return jax.shard_map(
        shards,
        mesh=mesh,
        in_specs=(
            P(None, both),
            P(both),
            P(both, None),
            P(None, both),
            P(both, None),
            P(both),
            P(both, None),
            P(both),
            P(both),
            P(both, None),
            P(both),
        ),
        out_specs=(P(None, both), P(None, both)),
        check_vma=False,
    )
```

profile of v0, /device:TPU:0, one launch (start us, length us, event | category | flops | bytes accessed | tf_op | source)
XLA Modules:
  0.0 44.5 jit_solution(7192933435052313342)
XLA Ops:
  0.6 0.0 copy-start.4
  0.6 0.0 copy-start.10
  0.7 0.7 %copy-done.4 = s32[2048]{0:T(1024)S(1)} copy-done((s32[2048]{0:T(1024)S(1)}, s32[2048]{0:T(1024)}, u32[]{:S(2)}) %copy-start.4) | copy-done | bytes 8216
  1.3 0.0 copy-done.10
  1.3 0.0 copy-start
  1.3 0.9 %copy-done = f32[27,2048]{1,0:T(8,128)S(1)} copy-done((f32[27,2048]{1,0:T(8,128)S(1)}, f32[27,2048]{1,0:T(8,128)}, u32[]{:S(2)}) %copy-start) | copy-done | bytes 221208
  2.3 0.0 copy-start.1
  2.3 0.8 %copy-done.1 = f32[3,4096]{1,0:T(4,128)S(1)} copy-done((f32[3,4096]{1,0:T(4,128)S(1)}, f32[3,4096]{1,0:T(4,128)}, u32[]{:S(2)}) %copy-start.1) | copy-done | bytes 49176
  3.1 0.0 copy-start.2
  3.1 0.7 %copy-done.2 = s32[4096,1]{0,1:T(1,128)S(1)} copy-done((s32[4096,1]{0,1:T(1,128)S(1)}, s32[4096,1]{0,1:T(1,128)}, u32[]{:S(2)}) %copy-start.2) | copy-done | bytes 16408
  3.8 0.0 copy-start.3
  3.8 0.7 %copy-done.3 = s32[4096]{0:T(1024)S(1)} copy-done((s32[4096]{0:T(1024)S(1)}, s32[4096]{0:T(1024)}, u32[]{:S(2)}) %copy-start.3) | copy-done | bytes 16408
  4.6 0.0 copy-start.5
  4.6 0.7 %copy-done.5 = s32[2048]{0:T(1024)S(1)} copy-done((s32[2048]{0:T(1024)S(1)}, s32[2048]{0:T(1024)}, u32[]{:S(2)}) %copy-start.5) | copy-done | bytes 8216
  5.3 0.0 copy-start.6
  5.3 0.7 %copy-done.6 = s32[2048,1]{0,1:T(1,128)S(1)} copy-done((s32[2048,1]{0,1:T(1,128)S(1)}, s32[2048,1]{0,1:T(1,128)}, u32[]{:S(2)}) %copy-start.6) | copy-done | bytes 8216
  6.0 0.0 copy-start.7
  6.0 0.7 %copy-done.7 = s32[2048]{0:T(1024)S(1)} copy-done((s32[2048]{0:T(1024)S(1)}, s32[2048]{0:T(1024)}, u32[]{:S(2)}) %copy-start.7) | copy-done | bytes 8216
  6.7 0.0 copy-start.8
  6.7 0.7 %copy-done.8 = s32[1,2048]{1,0:T(1,128)S(1)} copy-done((s32[1,2048]{1,0:T(1,128)S(1)}, s32[1,2048]{1,0:T(1,128)}, u32[]{:S(2)}) %copy-start.8) | copy-done | bytes 8216
  7.4 0.0 copy-start.9
  7.4 0.7 %copy-done.9 = f32[2048]{0:T(1024)S(1)} copy-done((f32[2048]{0:T(1024)S(1)}, f32[2048]{0:T(1024)}, u32[]{:S(2)}) %copy-start.9) | copy-done | bytes 8216
  8.0 35.1 %contact_step.1 = (f32[3,4096]{1,0:T(4,128)S(1)}, f32[27,2048]{1,0:T(8,128)S(1)}) custom-call(s32[1,32]{1,0:T(1,128)S(1)} %copy-done.10, f32[3,4096]{1,0:T(4,128)S(1)} %copy-done.1, s32[1,4096]{1,0:T(1,128)S(1)} %bitcast.7, s32[1,4096]{1,0:T(1,128)S(1)} %bitcast.8, f32[27,2048]{1,0:T(8,128)S(1)} %copy-done, s32[1,2048]{1,0:T(1,128)S(1)} %bitcast.9, ...), custom_call_target="tpu_custom_call" | custom-call | tf_op jit(solution)/shard_map/contact_step/pallas_call | solution.py:466
  43.2 0.6 %copy.15 = f32[3,4096]{1,0:T(4,128)} copy(f32[3,4096]{1,0:T(4,128)S(1)} %get-tuple-element.4) | data formatting | bytes 98304
  43.8 0.7 %copy.16 = f32[27,2048]{1,0:T(8,128)} copy(f32[27,2048]{1,0:T(8,128)S(1)} %get-tuple-element.5) | data formatting | bytes 442368
Async XLA Ops:
  0.6 0.7 %copy-start.4 = (s32[2048]{0:T(1024)S(1)}, s32[2048]{0:T(1024)}, u32[]{:S(2)}) copy-start(s32[2048]{0:T(1024)} %param.18) | copy-start | bytes 24580
  0.6 0.7 %copy-start.10 = (s32[1,32]{1,0:T(1,128)S(1)}, s32[1,32]{1,0:T(1,128)}, u32[]{:S(2)}) copy-start(s32[1,32]{1,0:T(1,128)} %refs_0_.1) | copy-start | bytes 388
  1.3 1.0 %copy-start = (f32[27,2048]{1,0:T(8,128)S(1)}, f32[27,2048]{1,0:T(8,128)}, u32[]{:S(2)}) copy-start(f32[27,2048]{1,0:T(8,128)} %refs_4_.1) | copy-start | bytes 663556
  2.3 0.8 %copy-start.1 = (f32[3,4096]{1,0:T(4,128)S(1)}, f32[3,4096]{1,0:T(4,128)}, u32[]{:S(2)}) copy-start(f32[3,4096]{1,0:T(4,128)} %refs_1_.1) | copy-start | bytes 147460
  3.1 0.7 %copy-start.2 = (s32[4096,1]{0,1:T(1,128)S(1)}, s32[4096,1]{0,1:T(1,128)}, u32[]{:S(2)}) copy-start(s32[4096,1]{0,1:T(1,128)} %param.15) | copy-start | bytes 49156
  3.8 0.7 %copy-start.3 = (s32[4096]{0:T(1024)S(1)}, s32[4096]{0:T(1024)}, u32[]{:S(2)}) copy-start(s32[4096]{0:T(1024)} %param.16) | copy-start | bytes 49156
  4.6 0.7 %copy-start.5 = (s32[2048]{0:T(1024)S(1)}, s32[2048]{0:T(1024)}, u32[]{:S(2)}) copy-start(s32[2048]{0:T(1024)} %param.19) | copy-start | bytes 24580
  5.3 0.7 %copy-start.6 = (s32[2048,1]{0,1:T(1,128)S(1)}, s32[2048,1]{0,1:T(1,128)}, u32[]{:S(2)}) copy-start(s32[2048,1]{0,1:T(1,128)} %param.20) | copy-start | bytes 24580
  6.0 0.7 %copy-start.7 = (s32[2048]{0:T(1024)S(1)}, s32[2048]{0:T(1024)}, u32[]{:S(2)}) copy-start(s32[2048]{0:T(1024)} %param.21) | copy-start | bytes 24580
  6.7 0.7 %copy-start.8 = (s32[1,2048]{1,0:T(1,128)S(1)}, s32[1,2048]{1,0:T(1,128)}, u32[]{:S(2)}) copy-start(s32[1,2048]{1,0:T(1,128)} %refs_9_.1) | copy-start | bytes 24580
  7.4 0.7 %copy-start.9 = (f32[2048]{0:T(1024)S(1)}, f32[2048]{0:T(1024)}, u32[]{:S(2)}) copy-start(f32[2048]{0:T(1024)} %param.12) | copy-start | bytes 24580
where the time goes:
time: 45.2 us; the launch traced here: 44.5 us
  Pallas kernels  35.1 us (78%)
  local copies, waits for them, and re-layouts  8.72 us (19%)
  between operations  0.67 us (1%)
    pallas_call x1, Pallas kernels, shards(): pl.pallas_call(functools.partial(step_kernel, n_mech, n_bin, ratio), out_...  35.1 us
    unnamed x24, local copies, waits for them, and re-layouts  8.72 us

commit v1 on v0

--- a/solution.py
+++ b/solution.py
@@ -74,9 +74,13 @@
     )
     onehot = hot(iota((lanes, width), 0) == lane.astype(jnp.int32))
     high, low = pieces(rows8)
-    return dot_lanes(by_group(key, high, groups).astype(BF16), onehot) + dot_lanes(
-        by_group(key, low, groups).astype(BF16), onehot
+    both = dot_lanes(
+        jnp.concatenate(
+            [by_group(key, high, groups).astype(BF16), by_group(key, low, groups).astype(BF16)], 0
+        ),
+        onehot,
     )
+    return both[: 4 * groups] + both[4 * groups :]
 
 
 def dispatch(n_bin, ratio, count, pos, sdest, sslot, send, info_s, faces):
@@ -207,33 +211,51 @@
     result = None
     for h in range(ref.shape[1] // LANES):
         line = jnp.broadcast_to(ref[row : row + 1, h * LANES : (h + 1) * LANES], (8, LANES))
-        value = jnp.take_along_axis(line, low, axis=1, mode="promise_in_bounds")
-        result = value if h == 0 else jnp.where(high == h, value, result)
+        value = [
+            jnp.take_along_axis(line, part, axis=1, mode="promise_in_bounds") for part in low
+        ]
+        if h == 0:
+            result = value
+        else:
+            result = [jnp.where(hi == h, v, r) for hi, v, r in zip(high, value, result)]
     return result
 
 
-def contact_block(first, dense, rows, order, coords, stiff, recv, ret, react, found, slot):
-    def far(c):
+def contact_blocks(blocks, rows, order, coords, stiff, recv, ret, react, found, slot):
+    def split(value):
+        return [value[8 * n : 8 * n + 8] for n in range(len(blocks))]
+
+    def far(first, c):
         return pl.ds(first + c, 8, stride=slot)
 
-    point = [recv[far(c), :] for c in range(3)]
-    code = recv[far(3), :]
+    def taken(c):
+        return jnp.concatenate([recv[far(first, c), :] for first, dense in blocks], 0)
+
+    def looked(ref, row, index):
+        low = split(index & (LANES - 1))
+        return jnp.concatenate(lookup(ref, row, low, split(index >> 7)), 0)
+
+    point = [taken(c) for c in range(3)]
+    code = taken(3)
     place = jnp.maximum(code - 1.0, 0.0).astype(jnp.int32)
-    face = lookup(order, 0, place & (LANES - 1), place >> 7)
-    low, high = face & (LANES - 1), face >> 7
-    nodes = [lookup(coords, r, low, high) for r in range(27)]
-    strength = jnp.where(code > 0.5, lookup(stiff, 0, low, high), 0.0)
-    found[pl.ds(dense, 8), :] = face
+    face = looked(order, 0, place)
+    nodes = [looked(coords, r, face) for r in range(27)]
+    strength = jnp.where(code > 0.5, looked(stiff, 0, face), 0.0)
     force, val_u, val_v = contact(point, nodes, strength)
-    for c in range(3):
-        ret[far(c), :] = force[c]
-    ret[far(3), :] = jnp.zeros_like(code)
+    for n, (first, dense) in enumerate(blocks):
+        part = slice(8 * n, 8 * n + 8)
+        found[pl.ds(dense, 8), :] = face[part]
+        for c in range(3):
+            ret[far(first, c), :] = force[c][part]
+        ret[far(first, 3), :] = jnp.zeros((8, LANES), F32)
     for j in range(3):
         for i in range(3):
             weight = -(val_u[i] * val_v[j])
             for c in range(3):
                 row = 3 * (i + 3 * j) + c
-                react[pl.ds(row * rows + dense, 8), :] = weight * force[c]
+                term = weight * force[c]
+                for n, (first, dense) in enumerate(blocks):
+                    react[pl.ds(row * rows + dense, 8), :] = term[8 * n : 8 * n + 8]
 
 
 def scatter(rows, high_count, react, found, total):
@@ -352,73 +374,87 @@
     for load in loads:
         load.wait()
     dispatch(n_bin, ratio, count, pos, sdest, sslot, send, info_s, faces)
-    dispatch_mirrors(n_bin, ratio, coords, mface, mnode, mdest, mslot, send, info_m)
     pl.semaphore_wait(barrier, devices - 1)
-
-    def go(i):
+    halves = ((0, 4 * ratio), (4 * ratio, 4))
+
+    def go(i, half):
         target = lax.rem(me + i, devices)
+        start, size = halves[half]
         return pltpu.make_async_remote_copy(
-            src_ref=send.at[target, pl.ds(0, used), :],
-            dst_ref=recv.at[pl.ds(pl.multiple_of(i * slot, slot), used), :],
-            send_sem=go_send.at[i],
-            recv_sem=go_recv.at[i],
+            src_ref=send.at[target, pl.ds(start, size), :],
+            dst_ref=recv.at[pl.ds(pl.multiple_of(i * slot, slot) + start, size), :],
+            send_sem=go_send.at[half, i],
+            recv_sem=go_recv.at[half, i],
             device_id=device(target),
             device_id_type=pl.DeviceIdType.MESH,
         )
 
-    def home(i):
+    def home(i, half):
         target = lax.rem(me - i + devices, devices)
+        start, size = halves[half]
         return pltpu.make_async_remote_copy(
-            src_ref=ret.at[pl.ds(pl.multiple_of(i * slot, slot), used), :],
-            dst_ref=back.at[me, pl.ds(0, used), :],
-            send_sem=home_send.at[i],
-            recv_sem=home_recv.at[i],
+            src_ref=ret.at[pl.ds(pl.multiple_of(i * slot, slot) + start, size), :],
+            dst_ref=back.at[me, pl.ds(start, size), :],
+            send_sem=home_send.at[half, i],
+            recv_sem=home_recv.at[half, i],
             device_id=device(target),
             device_id_type=pl.DeviceIdType.MESH,
         )
 
-    def start_go(i, carry):
-        go(i).start()
-        return carry
-
-    lax.fori_loop(1, devices, start_go, 0)
+    def start_go(half):
+        def start(i, carry):
+            go(i, half).start()
+            return carry
+
+        lax.fori_loop(1, devices, start, 0)
+
+    start_go(0)
+    dispatch_mirrors(n_bin, ratio, coords, mface, mnode, mdest, mslot, send, info_m)
+    start_go(1)
     recv[0:used, :] = send[me, 0:used, :]
     react[pl.ds(27 * rows, 5 * rows), :] = jnp.zeros((5 * rows, LANES), F32)
-
-    def group(j, carry):
-        for q in range(8):
-            i = j * 8 + q
+    tables = (rows, order, coords, stiff, recv, ret, react, found, slot)
+
+    def peers(j, count, act):
+        for q in range(count):
+            i = j * count + q
 
             @pl.when(i > 0)
             def _():
-                go(i).wait_recv()
-
-        def block(k, inside):
-            first = j * (8 * slot) + 4 * k
-            dense = pl.multiple_of((j * (ratio + 1) + k) * 8, 8)
-            contact_block(
-                first, dense, rows, order, coords, stiff, recv, ret, react, found, slot
-            )
-            return inside
-
-        lax.fori_loop(0, ratio + 1, block, 0)
-        for q in range(8):
-            i = j * 8 + q
-
-            @pl.when(i > 0)
-            def _():
-                home(i).start()
-
+                act(i)
+
+    def group(j, carry):
+        peers(j, 8, lambda i: go(i, 0).wait_recv())
+        blocks = [
+            (j * (8 * slot) + 4 * k, pl.multiple_of((j * ratio + k) * 8, 8)) for k in range(ratio)
+        ]
+        contact_blocks(blocks, *tables)
+        peers(j, 8, lambda i: home(i, 0).start())
         return carry
 
     lax.fori_loop(0, devices // 8, group, 0)
+    pair = 2 if devices % 16 == 0 else 1
+
+    def mirror_group(j, carry):
+        peers(j, 8 * pair, lambda i: go(i, 1).wait_recv())
+        blocks = []
+        for k in range(pair):
+            g = j * pair + k
+            dense = pl.multiple_of(ratio * devices + g * 8, 8)
+            blocks.append((g * (8 * slot) + 4 * ratio, dense))
+        contact_blocks(blocks, *tables)
+        peers(j, 8 * pair, lambda i: home(i, 1).start())
+        return carry
+
+    lax.fori_loop(0, devices // (8 * pair), mirror_group, 0)
     back[me, 0:used, :] = ret[0:used, :]
     scatter(rows, faces // LOW, react, found, total)
 
     def finish(i, carry):
-        go(i).wait_send()
-        home(i).wait_send()
-        home(i).wait_recv()
+        for half in range(2):
+            go(i, half).wait_send()
+            home(i, half).wait_send()
+            home(i, half).wait_recv()
         return carry
 
     lax.fori_loop(1, devices, finish, 0)
@@ -485,9 +521,9 @@
             pltpu.VMEM((80 * high_count, LOW), F32),
             pltpu.SemaphoreType.DMA((len(operands),)),
         ]
-        + [pltpu.SemaphoreType.DMA((devices,))] * 4,
+        + [pltpu.SemaphoreType.DMA((2, devices))] * 4,
         compiler_params=pltpu.CompilerParams(
-            vmem_limit_bytes=48 * 2**20, collective_id=0, has_side_effects=True
+            vmem_limit_bytes=63 * 2**20, collective_id=0, has_side_effects=True
         ),
         name="contact_step",
     )(*operands)

time: 45.2 us -> 42.9 us (0.949); the launches traced: 44.5 us -> 42.7 us
  local copies, waits for them, and re-layouts: 8.72 us -> 3.15 us
  Pallas kernels: 35.1 us -> 38.9 us
    unnamed x24 -> x2, local copies, waits for them, and re-layouts: 8.72 us -> 3.15 us
    pallas_call x1, Pallas kernels: 35.1 us -> 38.9 us  [shards(): pl.pallas_call(functools.partial(step_kernel, n_mech, n_bin, ratio), out_...]
where the time goes in v1:
time: 42.9 us; the launch traced here: 42.7 us
  Pallas kernels  38.9 us (91%)
  local copies, waits for them, and re-layouts  3.15 us (7%)
  between operations  0.64 us (1%)
    pallas_call x1, Pallas kernels, shards(): pl.pallas_call(functools.partial(step_kernel, n_mech, n_bin, ratio), out_...  38.9 us
    unnamed x2, local copies, waits for them, and re-layouts  3.15 us

profile of v1, /device:TPU:0, one launch (start us, length us, event | category | flops | bytes accessed | tf_op | source)
XLA Modules:
  0.0 42.7 jit_solution(610528940011512872)
XLA Ops:
  0.6 38.9 %contact_step.1 = (f32[3,4096]{1,0:T(4,128)}, f32[27,2048]{1,0:T(8,128)}) custom-call(s32[1,32]{1,0:T(1,128)} %refs_0_.1, f32[3,4096]{1,0:T(4,128)} %refs_1_.1, s32[1,4096]{1,0:T(1,128)} %bitcast.7, s32[1,4096]{1,0:T(1,128)} %bitcast.8, f32[27,2048]{1,0:T(8,128)} %refs_4_.1, s32[1,2048]{1,0:T(1,128)} %bitcast.9, s32[1,2048]{1,0:T(1,128)} %bitcast.10, ...), custom_call_target="tpu_custom_call" | custom-call | tf_op jit(solution)/shard_map/contact_step/pallas_call | solution.py:502
  39.5 1.5 %copy.15 = f32[3,4096]{1,0:T(4,128)} copy(f32[3,4096]{1,0:T(4,128)} %get-tuple-element.4) | data formatting | bytes 98304
  41.0 1.7 %copy.16 = f32[27,2048]{1,0:T(8,128)} copy(f32[27,2048]{1,0:T(8,128)} %get-tuple-element.5) | data formatting | bytes 442368

commit v2 on v1

--- a/solution.py
+++ b/solution.py
@@ -30,6 +30,16 @@
 
 def hot(mask):
     return jnp.where(mask, 1.0, 0.0).astype(BF16)
+
+
+def counted(shape):
+    return iota(shape, 0).astype(F32).astype(BF16)
+
+
+def hot_rows(numbers, row):
+    wide = jnp.broadcast_to(row.astype(F32), (16, row.shape[1])).astype(BF16)
+    wide = jnp.concatenate([wide] * (numbers.shape[0] // 16), 0)
+    return jnp.where(numbers == wide, jnp.ones_like(wide), jnp.zeros_like(wide))
 
 
 def dot_lanes(left, right):
@@ -62,8 +72,12 @@
 
 def by_group(key, rows8, groups):
     width = rows8.shape[1]
-    group = (iota((4 * groups, width), 0) >> 2).astype(F32)
-    return jnp.where(group == key, jnp.concatenate([rows8] * (groups // 2), 0), 0.0)
+    group = (iota((4 * groups, width), 0) >> 2).astype(F32).astype(BF16)
+    wide = jnp.broadcast_to(key, (16, width)).astype(BF16)
+    wide = jnp.concatenate([wide] * (groups // 4), 0)
+    rows16 = jnp.concatenate([rows8, rows8], 0).astype(BF16)
+    rows16 = jnp.concatenate([rows16] * (groups // 4), 0)
+    return jnp.where(group == wide, rows16, jnp.zeros_like(rows16))
 
 
 def spread(key, lane, point, index, groups, lanes):
@@ -72,11 +86,11 @@
     rows8 = jnp.where(
         row == 0, point[0], jnp.where(row == 1, point[1], jnp.where(row == 2, point[2], index))
     )
-    onehot = hot(iota((lanes, width), 0) == lane.astype(jnp.int32))
+    onehot = hot_rows(counted((lanes, width)), lane)
     high, low = pieces(rows8)
     both = dot_lanes(
         jnp.concatenate(
-            [by_group(key, high, groups).astype(BF16), by_group(key, low, groups).astype(BF16)], 0
+            [by_group(key, high, groups), by_group(key, low, groups)], 0
         ),
         onehot,
     )
@@ -144,7 +158,7 @@
         info_m[0:1, cols] = owner
         info_m[1:2, cols] = rank
         face = mface[:, cols]
-        onehot = hot(iota((LOW, width), 0) == (face & (LOW - 1)))
+        onehot = hot_rows(counted((LOW, width)), face & (LOW - 1))
         found = dot_plain(table, jnp.concatenate([onehot, onehot], 0))
         part = face >> 8
         nodes = jnp.zeros((32, width), F32)
@@ -263,19 +277,20 @@
 
     def add(i, carry):
         lefts, rights = [], []
+        numbers = counted((LOW, LANES))
         for q in range(8):
             p = i * 8 + q
             value = react[pl.ds(p, 32, stride=rows), :]
             upper, lower = pieces(value)
             both = jnp.concatenate([upper.astype(BF16), lower.astype(BF16)], 0)
             face = found[pl.ds(p, 1), :]
-            high = jnp.broadcast_to(face >> 8, (16, LANES))
+            high = jnp.broadcast_to((face >> 8).astype(F32), (16, LANES)).astype(BF16)
+            high = jnp.concatenate([high] * 4, 0)
             parts = []
             for h in range(high_count):
-                mask = hot(high == h)
-                parts.append(both * jnp.concatenate([mask] * 4, 0))
+                parts.append(jnp.where(high == float(h), both, jnp.zeros_like(both)))
             lefts.append(jnp.concatenate(parts, 0))
-            rights.append(hot(iota((LOW, LANES), 0) == (face & (LOW - 1))))
+            rights.append(hot_rows(numbers, face & (LOW - 1)))
         total[...] += dot_lanes(jnp.concatenate(lefts, 1), jnp.concatenate(rights, 1))
         return carry
 
@@ -284,7 +299,7 @@
 
 def fetch(key, lane, table, groups):
     width = key.shape[1]
-    onehot = hot(iota((LANES, width), 0) == lane.astype(jnp.int32))
+    onehot = hot_rows(counted((LANES, width)), lane)
     spreaded = dot_plain(table, jnp.concatenate([onehot, onehot], 0))
     group = (iota((4 * groups, width), 0) >> 2).astype(F32)
     spreaded = jnp.where(group == key, spreaded, 0.0)
@@ -316,7 +331,7 @@
                 for j in range(5):
                     left.append(jnp.where(rel == 16 * h + 2 * j, piece, 0.0))
         left = jnp.concatenate(left, 0).astype(BF16)
-        onehot = hot(iota((LOW, width), 0) == (face & (LOW - 1)))
+        onehot = hot_rows(counted((LOW, width)), face & (LOW - 1))
         term = dot_lanes(left, onehot)
         acc = term if acc is None else acc + term
     own[...] = acc
@@ -371,7 +386,7 @@
     lax.fori_loop(1, devices, greet, 0)
     (count, pos, sdest, sslot, coords, mface, mnode, mdest, mslot, order, stiff) = local
     faces = coords.shape[1]
-    for load in loads:
+    for load in loads[:4]:
         load.wait()
     dispatch(n_bin, ratio, count, pos, sdest, sslot, send, info_s, faces)
     pl.semaphore_wait(barrier, devices - 1)
@@ -409,6 +424,8 @@
         lax.fori_loop(1, devices, start, 0)
 
     start_go(0)
+    for load in loads[4:]:
+        load.wait()
     dispatch_mirrors(n_bin, ratio, coords, mface, mnode, mdest, mslot, send, info_m)
     start_go(1)
     recv[0:used, :] = send[me, 0:used, :]

time: 42.9 us -> 42.5 us (level)
    pallas_call x1, Pallas kernels: 38.9 us -> 38.5 us  [shards(): pl.pallas_call(functools.partial(step_kernel, n_mech, n_bin, ratio), out_...]
where the time goes in v2:
time: 42.5 us; the launch traced here: 42.3 us
  Pallas kernels  38.5 us (91%)
  local copies, waits for them, and re-layouts  3.15 us (7%)
  between operations  0.64 us (2%)
    pallas_call x1, Pallas kernels, shards(): pl.pallas_call(functools.partial(step_kernel, n_mech, n_bin, ratio), out_...  38.5 us
    unnamed x2, local copies, waits for them, and re-layouts  3.15 us

profile of v2, /device:TPU:0, one launch (start us, length us, event | category | flops | bytes accessed | tf_op | source)
XLA Modules:
  0.0 42.3 jit_solution(16001361207272630512)
XLA Ops:
  0.6 38.5 %contact_step.1 = (f32[3,4096]{1,0:T(4,128)}, f32[27,2048]{1,0:T(8,128)}) custom-call(s32[1,32]{1,0:T(1,128)} %refs_0_.1, f32[3,4096]{1,0:T(4,128)} %refs_1_.1, s32[1,4096]{1,0:T(1,128)} %bitcast.7, s32[1,4096]{1,0:T(1,128)} %bitcast.8, f32[27,2048]{1,0:T(8,128)} %refs_4_.1, s32[1,2048]{1,0:T(1,128)} %bitcast.9, s32[1,2048]{1,0:T(1,128)} %bitcast.10, ...), custom_call_target="tpu_custom_call" | custom-call | tf_op jit(solution)/shard_map/contact_step/pallas_call | solution.py:519
  39.1 1.5 %copy.15 = f32[3,4096]{1,0:T(4,128)} copy(f32[3,4096]{1,0:T(4,128)} %get-tuple-element.4) | data formatting | bytes 98304
  40.6 1.7 %copy.16 = f32[27,2048]{1,0:T(8,128)} copy(f32[27,2048]{1,0:T(8,128)} %get-tuple-element.5) | data formatting | bytes 442368
